TPU v7x, 256 devices: a whole 4x4x8 slice. The times are simulated.
256 devices in a mesh: ia: 16 (over z_hi, y, core), ja: 4 (over x), ka: 4 (over z_lo).
Axes of the slice: x: 4, y: 4, z: 8 (z_hi: 2, z_lo: 4; z = z_hi * 4 + z_lo), core: 2. Of those that a mesh axis runs over, the one named last changes fastest.
Arguments:
- tensor: float32 [256, 256, 8192], P('ia', 'ka', 'ja'), may hold values from -6 to 6
- factor_b: float32 [8192, 64], P(('ja', 'ka')), may hold values from -1 to 1
- factor_c: float32 [256, 64], P('ka'), may hold values from -1 to 1
Outputs:
- factor_a: float32 [256, 64], P(('ia', 'ja', 'ka'))
- mode_two: float32 [64, 4, 2048], P(None, 'ja', ('ia', 'ka'))
All inputs are finite; a program needn't handle non-finite values.
Results may differ from a plain program's by a relative error of at most 0.00026.
Values sent between devices are 32-bit elements; how exact they have to be, the bound alone decides.
A program may use at most 64 MiB of HBM per device.

v0:
```python
import jax
import jax.numpy as jnp
from jax import lax
from jax.sharding import PartitionSpec as P


def body(tensor, factor_b, factor_c):
    highest = lax.Precision.HIGHEST
    factor_rank = factor_c.shape[1]
    column_block = tensor.shape[2]
    local_b = jnp.dot(factor_b.T, factor_b, precision=highest, preferred_element_type=jnp.float32)
    local_c = jnp.dot(factor_c.T, factor_c, precision=highest, preferred_element_type=jnp.float32)
    gram_b = lax.psum(local_b, ("ja", "ka"))
    gram_c = lax.psum(local_c, "ka")
    triangle = jnp.linalg.cholesky(gram_b * gram_c)
    partial_value = jnp.einsum("ikj,kr->rij", tensor, factor_c, precision=highest)
    mode_one = jnp.einsum(
        "rij,jr->ir",
        partial_value,
        lax.all_gather(factor_b, "ka", axis=0, tiled=True),
        precision=highest,
    )
    empty_two = jnp.zeros((factor_rank, column_block), jnp.float32)
    own_rows = lax.psum_scatter(mode_one, ("ja", "ka"), scatter_dimension=0, tiled=True)
    a_rows = jax.scipy.linalg.cho_solve((triangle, True), own_rows.T).T
    contracted = jnp.einsum("ikj,kr->rij", tensor, factor_c, precision=highest)
    mode_partial = empty_two + jnp.einsum(
        "rij,ir->rj",
        contracted,
        lax.all_gather(a_rows, ("ja", "ka"), axis=0, tiled=True),
        precision=highest,
    )
    reduced = lax.psum_scatter(mode_partial, ("ia", "ka"), scatter_dimension=1, tiled=True)
    return (a_rows, reduced.reshape(factor_rank, 1, reduced.shape[1]))


def solution(mesh):
    placed = (P("ia", "ka", "ja"), P(("ja", "ka"), None), P("ka", None))
    return jax.shard_map(
        body,
        mesh=mesh,
        in_specs=placed,
        out_specs=(P(("ia", "ja", "ka"), None), P(None, "ja", ("ia", "ka"))),
        check_vma=False,
    )
```

profile of v0, /device:TPU:1, one launch (start us, length us, event | category | flops | bytes accessed | tf_op | source)
XLA Modules:
  0.0 469.4 jit_solution(18143469443834605762)
XLA Ops:
  7.2 0.0 copy-start
  7.2 0.0 reduce-scatter.2.cloned.1.call-start
  7.2 16.5 %all_gather.6 = f32[2048,64]{0,1:T(8,128)S(1)} all-gather(f32[512,64]{0,1:T(8,128)} %param.4), channel_id=1, replica_groups=mesh['ia'=16,'ja'=4,'ka'=4] {'ka'}, dimensions={0}, use_global_device_ids=true | all-gather | bytes 655360 | tf_op jit(solution)/shard_map/all_gather | solution.py:20
  23.8 1.2 fusion.12
  25.0 0.0 copy-done
  25.0 0.2 fusion.13
  25.3 10.2 %fusion.4 = f32[64,16,2048]{2,0,1:T(8,128)S(1)} fusion(f32[16,64,2048]{2,1,0:T(8,128)} %param.3, f32[64,64]{1,0:T(8,128)S(1)} %copy-done), kind=kOutput, calls=%fused_computation.7 | convolution fusion | flops 1610612736 | bytes 16793600 | tf_op jit(solution)/shard_map/ikj,kr->rij/dot_general | solution.py:16
  35.5 0.0 copy-start.1
  35.5 0.0 copy-start.2
  35.5 3.2 copy-done.1
  38.7 14.4 %fusion = f32[64,1,16]{2,1,0:T(1,128)S(1)} fusion(f32[64,16,2048]{2,0,1:T(8,128)S(1)} %fusion.4, f32[2048,64,1]{0,1,2:T(8,128)S(1)} %bitcast.37), kind=kOutput, calls=%fused_computation.1 | convolution fusion | flops 25165824 | bytes 8916992 | tf_op jit(solution)/shard_map/rij,jr->ir/dot_general | solution.py:17
  53.1 0.1 copy.18
  53.1 13.8 %psum.15 = f32[64,64]{0,1:T(8,128)S(1)} all-reduce(f32[64,64]{0,1:T(8,128)S(1)} %fusion.13), channel_id=1, replica_groups=mesh['ia'=16,'ja'=4,'ka'=4] {'ka'}, use_global_device_ids=true, to_apply=%region_1.0 | all-reduce | flops 4096 | bytes 32768 | tf_op jit(solution)/shard_map/psum | solution.py:14
  66.9 62.8 %all-reduce.2 = (f32[64,64]{0,1:T(8,128)S(1)}, f32[16,64]{1,0:T(8,128)S(1)}) all-reduce(f32[64,64]{0,1:T(8,128)S(1)} %fusion.12, f32[16,64]{1,0:T(8,128)S(1)} %bitcast.39), channel_id=1, replica_groups=mesh['ia'=16,'ja'=4,'ka'=4] {'ja','ka'}, use_global_device_ids=true, to_apply=%region_0.0 | all-reduce | flops 5120 | bytes 40960 | tf_op jit(solution)/shard_map/psum | solution.py:13
  129.7 0.1 copy.11
  129.8 5.8 %cholesky.16 = f32[64,64]{1,0:T(8,128)S(1)} custom-call(f32[64,64]{1,0:T(8,128)S(1)} %fusion.9), custom_call_target="Cholesky" | custom-call | tf_op jit(solution)/shard_map/jit(cholesky)/cholesky | solution.py:15
  135.7 0.6 compare_reduce_fusion
  136.3 0.7 fusion.3
  137.0 4.9 %custom-call.10 = f32[1,64,64]{1,2,0:T(8,128)S(1)} custom-call(f32[1,64,64]{2,1,0:T(8,128)S(1)} %fusion.3), custom_call_target="InvertDiagBlocksLowerTriangular" | custom-call | tf_op jit(solution)/shard_map/jit(_cho_solve)/triangular_solve | solution.py:25
  141.9 0.0 copy-done.2
  141.9 0.6 fusion.11
  142.5 0.8 convolution_bitcast_fusion
  143.3 0.2 fusion.6
  143.4 0.0 copy-start.3
  144.1 0.1 bitcast_dynamic-update-slice_fusion
  144.3 31.1 %all-reduce = f32[1024]{0:T(1024)S(1)} all-reduce(f32[1024]{0:T(1024)S(1)} %bitcast_dynamic-update-slice_fusion), channel_id=2, replica_groups=mesh['ia'=16,'ja'=4,'ka'=4] {'ja','ka'}, use_global_device_ids=true, to_apply=%add | all-reduce | flops 1024 | bytes 8192
  175.3 0.1 reshape.31
  175.4 4.0 multiply_reduce_fusion
  179.5 1.3 copy.23
  180.8 0.0 reduce-scatter.2.cloned.1.call-update
  180.8 281.7 %reduce-scatter.2.cloned.1.call-done = f32[64,32]{0,1:T(8,128)} async-done(((f32[64,2048]{0,1:T(8,128)}), f32[64,32]{0,1:T(8,128)}) %reduce-scatter.2.cloned.1.call-update) | async-done | bytes 8208 | tf_op jit(solution)/shard_map/reduce_scatter | solution.py:33
  462.5 0.0 copy-done.3
  (4 shorter events, 0.0 us)
Async XLA Ops:
  7.2 17.9 %copy-start = (f32[64,64]{1,0:T(8,128)S(1)}, f32[64,64]{1,0:T(8,128)}, u32[]{:S(2)}) copy-start(f32[64,64]{1,0:T(8,128)} %param.5) | copy-start | bytes 49156
  7.2 455.4 %reduce-scatter.2.cloned.1.call-start = ((), (), s32[]{:S(2)}) async-start(), calls=%async_computation.1 | async-start | bytes 1064960 | tf_op jit(solution)/shard_map/reduce_scatter | solution.py:33
  35.5 3.2 copy-start.1
  35.5 106.4 %copy-start.2 = (u32[256]{0:T(256)S(1)}, u32[256]{0:T(256)}, u32[]{:S(2)}) copy-start(u32[256]{0:T(256)} %constant.51) | copy-start | bytes 3076
  143.4 319.1 %copy-start.3 = (f32[1,64]{1,0:T(1,128)}, f32[1,64]{1,0:T(1,128)S(1)}, u32[]{:S(2)}) copy-start(f32[1,64]{1,0:T(1,128)S(1)} %fusion.6) | copy-start | bytes 772
Sparse Core Ops, SparseCore 0:
  180.9 281.5 reduce-scatter.1
where the time goes:
time: 473 us; the launch traced here: 469 us
  waiting for transfers between devices  282 us (60%)
  blocking collectives  124 us (26%)
  matrix products  27 us (6%)
  other arithmetic  16.1 us (3%)
  between operations  14.8 us (3%)
  local copies, waits for them, and re-layouts  5.48 us (1%)
    reduce_scatter x1, waiting for transfers between devices, body(): lax.psum_scatter(mode_partial, ('ia', 'ka'), scatter_dimension=1, tiled=T...  282 us
    psum x1, blocking collectives, body(): gram_b = lax.psum(local_b, ('ja', 'ka'))  62.8 us
    unnamed x1, blocking collectives  31.1 us
    all_gather x1, blocking collectives, body(): lax.all_gather(factor_b, 'ka', axis=0, tiled=True)  16.5 us
    dot_general x1, matrix products, body(): jnp.einsum('rij,jr->ir', partial_value, lax.all_gather(factor_b, 'ka', ax...  14.4 us
    psum x1, blocking collectives, body(): gram_c = lax.psum(local_c, 'ka')  13.8 us
    dot_general x1, matrix products, body(): jnp.einsum('ikj,kr->rij', tensor, factor_c, precision=highest)  10.2 us
  transfers between devices with their start and end apart: 1, of which 1 were waited for; matrix products, arithmetic and copies ran while one was open for 0% of the time, Pallas kernels for 0%

commit v1 on v0

v1 whole, which is shorter than its diff:
```python
import jax
import jax.numpy as jnp
from jax import lax
from jax.experimental import pallas as pl
from jax.experimental.pallas import tpu as pltpu
from jax.sharding import PartitionSpec as P

MESH = pl.DeviceIdType.MESH
F32 = jnp.float32
BF16 = jnp.bfloat16
HIGHEST = lax.Precision.HIGHEST

R = 64
NI = 16
NK = 64
NT = 16
LANES = 128
NX, NY, NZ, NZLO = 4, 4, 8, 4
EARLY = 4
MIDDLE = 10


def place(x, y, z, core):
    return (((z // NZLO) * NY + y) * 2 + core, x, z % NZLO)


def kernel(
    tensor,
    b_ref,
    c_ref,
    a_out,
    two_out,
    rows,
    partial,
    c_wide,
    gram_own,
    gram_x,
    gram_mid,
    gram_z,
    b_near,
    b_far,
    one_acc,
    one_own,
    one_recv,
    h_inv,
    a_wide,
    a_rows,
    pair_send,
    pair_recv,
    packed,
    two_recv,
    t_sem,
    b_send,
    b_recv_sem,
    gx_send,
    gx_recv,
    gz_send,
    gz_recv,
    one_send,
    one_recv_sem,
    pair_ssem,
    pair_rsem,
    two_send,
    two_recv_sem,
):
    ia = lax.axis_index("ia")
    x = lax.axis_index("ja")
    zlo = lax.axis_index("ka")
    core = ia % 2
    y = (ia // 2) % NY
    zhi = ia // (2 * NY)
    z = zhi * NZLO + zlo

    def at_z(d):
        return place(x, y, (z + d + NZ) % NZ, core)

    def at_x(d):
        return place((x + d) % NX, y, z, core)

    other_core = place(x, y, z, 1 - core)

    def remote(src, dst, send, recv, target):
        copy = pltpu.make_async_remote_copy(
            src_ref=src, dst_ref=dst, send_sem=send, recv_sem=recv, device_id=target, device_id_type=MESH
        )
        return copy

    def load_row(i):
        return pltpu.make_async_copy(tensor.at[i], rows.at[i], t_sem.at[i])

    for i in range(NI):
        load_row(i).start()

    barrier = pltpu.get_barrier_semaphore()
    peers = [other_core]
    peers += [at_x(d) for d in range(1, NX)]
    peers += [place(x, (y + d) % NY, z, core) for d in range(1, NY)]
    peers += [at_z(d) for d in range(1, NZ)]
    for peer in peers:
        pl.semaphore_signal(barrier, inc=1, device_id=peer, device_id_type=MESH)

    c_t = c_ref[...].T
    c_hi = c_t.astype(BF16)
    c_lo = (c_t - c_hi.astype(F32)).astype(BF16)
    c_wide[...] = jnp.concatenate([c_hi, c_lo, c_hi, c_lo], axis=1)
    b_own = b_ref[...]
    gram_b = lax.dot_general(b_own, b_own, (((1,), (1,)), ((), ())), precision=HIGHEST, preferred_element_type=F32)
    gram_c = lax.dot_general(c_t, c_t, (((1,), (1,)), ((), ())), precision=HIGHEST, preferred_element_type=F32)
    gram_own[...] = jnp.concatenate([gram_b, gram_c], axis=1)

    def contract(i, carry):
        load_row(i).wait()
        for chunk in range(4):
            values = rows[i, :, pl.ds(chunk * 512, 512)]
            hi = values.astype(BF16)
            lo = (values - hi.astype(F32)).astype(BF16)
            out = jnp.dot(c_wide[...], jnp.concatenate([hi, hi, lo, lo], axis=0), preferred_element_type=F32)
            for part in range(4):
                partial[chunk * 4 + part, i] = out[:, part * LANES : (part + 1) * LANES]
        return carry

    lax.fori_loop(0, EARLY, contract, 0)

    pl.semaphore_wait(barrier, len(peers))

    half = b_ref.shape[1] // 2
    b_copies = [
        remote(b_ref.at[:, pl.ds(0, half)], b_far.at[0], b_send.at[2], b_recv_sem.at[2], at_z(2)),
        remote(b_ref.at[:, pl.ds(half, half)], b_far.at[1], b_send.at[3], b_recv_sem.at[3], at_z(-2)),
        remote(b_ref, b_near.at[0], b_send.at[0], b_recv_sem.at[0], at_z(1)),
        remote(b_ref, b_near.at[1], b_send.at[1], b_recv_sem.at[1], at_z(-1)),
    ]
    gx_copies = [remote(gram_own, gram_x.at[d - 1], gx_send.at[d - 1], gx_recv.at[d - 1], at_x(d)) for d in range(1, NX)]
    for copy in gx_copies + b_copies:
        copy.start()

    lax.fori_loop(EARLY, MIDDLE, contract, 0)

    for copy in gx_copies:
        copy.wait_recv()
    own = gram_own[...]
    total = own + gram_x[0] + gram_x[1] + gram_x[2]
    lane = lax.broadcasted_iota(jnp.int32, (R, LANES), 1)
    gram_mid[...] = jnp.where(lane < R, total, own)
    gz_copies = [
        remote(gram_mid, gram_z.at[n], gz_send.at[n], gz_recv.at[n], at_z(d)) for n, d in enumerate((2, 1, -1))
    ]
    for copy in gz_copies:
        copy.start()

    lax.fori_loop(MIDDLE, NI, contract, 0)

    def first_block(i, carry):
        acc = jnp.zeros((R, LANES), F32)
        for part in range(4):
            acc += partial[zlo * 4 + part, i] * b_ref[:, part * LANES : (part + 1) * LANES]
        one_acc[i] = acc
        return carry

    lax.fori_loop(0, NI, first_block, 0)

    b_copies[2].wait_recv()
    b_copies[3].wait_recv()
    before = (zlo + 3) % NZLO
    after = (zlo + 1) % NZLO
    across = (zlo + 2) % NZLO

    def near_blocks(i, carry):
        acc = one_acc[i]
        for part in range(4):
            acc += partial[before * 4 + part, i] * b_near[0, :, part * LANES : (part + 1) * LANES]
            acc += partial[after * 4 + part, i] * b_near[1, :, part * LANES : (part + 1) * LANES]
        one_acc[i] = acc
        return carry

    lax.fori_loop(0, NI, near_blocks, 0)

    b_copies[0].wait_recv()
    b_copies[1].wait_recv()
    lane8 = lax.broadcasted_iota(jnp.int32, (8, LANES), 1)

    def far_block(i, carry):
        acc = one_acc[i]
        for part in range(4):
            acc += (
                partial[across * 4 + part, i]
                * b_far[part // 2, :, (part % 2) * LANES : (part % 2 + 1) * LANES]
            )
        for g in range(8):
            total = jnp.sum(acc[g * 8 : (g + 1) * 8], axis=1, keepdims=True)
            carry = jnp.where(lane8 == g * NI + i, total, carry)
        return carry

    one_own[...] = lax.fori_loop(0, NI, far_block, jnp.zeros((8, LANES), F32))

    one_targets = [((3 - n // NZLO), (3 - n % NZLO)) for n in range(NX * NZLO - 1)]
    for n, (dx, dz) in enumerate(one_targets):
        target = place((x + dx) % NX, y, zhi * NZLO + (zlo + dz) % NZLO, core)
        remote(one_own, one_recv.at[n], one_send, one_recv_sem, target).start()

    for copy in gz_copies:
        copy.wait_recv()
    grams = gram_mid[...] + gram_z[0] + gram_z[1] + gram_z[2]
    product = grams * pltpu.roll(grams, R, 1)
    row_id = lax.broadcasted_iota(jnp.int32, (R, LANES), 0)
    work = jnp.where(lane < R, product, jnp.where(lane == row_id + R, 1.0, 0.0))
    groups = [work[g * 8 : (g + 1) * 8] for g in range(8)]
    sub = lax.broadcasted_iota(jnp.int32, (8, LANES), 0)
    for p in range(R):
        gp, s = p // 8, p % 8
        row = groups[gp][s : s + 1]
        scale = lax.rsqrt(row[:, p : p + 1])
        unit = row * scale
        for g in range(gp, 8):
            column = groups[g][:, p : p + 1] * scale
            update = groups[g] - column * unit
            if g == gp:
                update = jnp.where(sub > s, update, jnp.where(sub == s, unit, groups[g]))
            groups[g] = update
    lower_inv = jnp.concatenate(groups, axis=0)[:, R:]
    h_inv[...] = lax.dot_general(
        lower_inv, lower_inv, (((0,), (0,)), ((), ())), precision=HIGHEST, preferred_element_type=F32
    )

    pltpu.make_async_copy(one_recv, one_recv, one_recv_sem).wait()
    mode_one = one_own[...]
    for n in range(NX * NZLO - 1):
        mode_one = mode_one + one_recv[n]
    mode_one_t = jnp.concatenate(
        [mode_one if g == 0 else pltpu.roll(mode_one, LANES - g * NI, 1) for g in range(8)], axis=0
    )
    a_t = jnp.dot(h_inv[...], mode_one_t, precision=HIGHEST, preferred_element_type=F32)
    for i in range(NI):
        a_wide[i] = jnp.broadcast_to(a_t[:, i : i + 1], (R, LANES))

    def combine(tile):
        acc = partial[tile, 0] * a_wide[0]
        for i in range(1, NI):
            acc += partial[tile, i] * a_wide[i]
        return acc

    def block_of(n):
        return ((zhi + 1 + n // NY) % 2, (y + 2 + n) % NY)

    def pair_copy(n):
        return remote(pair_send.at[n], pair_recv.at[n], pair_ssem.at[n], pair_rsem.at[n], other_core)

    def for_other_core(n, carry):
        to_zhi, to_y = block_of(n)
        pair_send[n] = combine((to_zhi * NY + to_y) * 2 + 1 - core)
        pair_copy(n).start()
        return carry

    lax.fori_loop(0, 8, for_other_core, 0)

    lane16 = lax.broadcasted_iota(jnp.int32, (16, LANES), 1) // 32

    def reduce_pair(n):
        to_zhi, to_y = block_of(n)
        value = combine((to_zhi * NY + to_y) * 2 + core)
        pair_copy(n).wait_recv()
        value = value + pair_recv[n]
        for to_zlo in range(NZLO):
            block = value[0:16] if to_zlo == 0 else pltpu.roll(value[0:16], LANES - 32 * to_zlo, 1)
            for g in range(1, 4):
                piece = value[g * 16 : (g + 1) * 16]
                shift = (32 * (g - to_zlo)) % LANES
                block = jnp.where(lane16 == g, pltpu.roll(piece, shift, 1) if shift else piece, block)
            packed[n, to_zlo] = block

    def send_block(n, step):
        to_zhi, to_y = block_of(n)
        to_zlo = (zlo + step) % NZLO
        slot = n * NZLO + step - 1
        remote(
            packed.at[n, to_zlo],
            two_recv.at[slot],
            two_send,
            two_recv_sem,
            place(x, to_y, to_zhi * NZLO + to_zlo, core),
        ).start()

    def far_blocks(n, carry):
        reduce_pair(n)
        for step in (2, 1, 3, 4):
            send_block(n, step)
        return carry

    lax.fori_loop(0, 6, far_blocks, 0)
    lax.fori_loop(7, 8, far_blocks, 0)
    reduce_pair(6)
    for step in (2, 1, 3):
        send_block(6, step)

    a_rows[...] = a_t.T
    a_out[...] = a_rows[pl.ds(x * NZLO + zlo, 1), :]

    two_recv[6 * NZLO + 3] = packed[6, zlo]
    pltpu.make_async_copy(two_recv.at[pl.ds(0, 31)], two_recv.at[pl.ds(0, 31)], two_recv_sem).wait()

    def add_block(n, acc):
        return acc + two_recv[n]

    total = lax.fori_loop(0, 32, add_block, jnp.zeros((16, LANES), F32))
    columns = jnp.concatenate([total if g == 0 else pltpu.roll(total, LANES - 32 * g, 1) for g in range(4)], axis=0)
    two_out[...] = columns.T[0:32]

    for copy in b_copies + gx_copies + gz_copies:
        copy.wait_send()
    pltpu.make_async_copy(one_recv, one_recv, one_send).wait()

    def pair_done(n, carry):
        pair_copy(n).wait_send()
        return carry

    lax.fori_loop(0, 8, pair_done, 0)
    pltpu.make_async_copy(two_recv.at[pl.ds(0, 31)], two_recv.at[pl.ds(0, 31)], two_send).wait()


def body(tensor, factor_b, factor_c):
    dma = pltpu.SemaphoreType.DMA
    vmem = pl.BlockSpec(memory_space=pltpu.VMEM)
    a_rows, two = pl.pallas_call(
        kernel,
        name="cp_step",
        out_shape=(jax.ShapeDtypeStruct((1, R), F32), jax.ShapeDtypeStruct((32, R), F32)),
        in_specs=[pl.BlockSpec(memory_space=pltpu.HBM), vmem, vmem],
        out_specs=(vmem, vmem),
        scratch_shapes=[
            pltpu.VMEM((NI, NK, NT * LANES), F32),
            pltpu.VMEM((NT, NI, R, LANES), F32),
            pltpu.VMEM((R, 4 * NK), BF16),
            pltpu.VMEM((R, LANES), F32),
            pltpu.VMEM((3, R, LANES), F32),
            pltpu.VMEM((R, LANES), F32),
            pltpu.VMEM((3, R, LANES), F32),
            pltpu.VMEM((2, R, 512), F32),
            pltpu.VMEM((2, R, 256), F32),
            pltpu.VMEM((NI, R, LANES), F32),
            pltpu.VMEM((8, LANES), F32),
            pltpu.VMEM((15, 8, LANES), F32),
            pltpu.VMEM((R, R), F32),
            pltpu.VMEM((NI, R, LANES), F32),
            pltpu.VMEM((LANES, R), F32),
            pltpu.VMEM((8, R, LANES), F32),
            pltpu.VMEM((8, R, LANES), F32),
            pltpu.VMEM((8, NZLO, 16, LANES), F32),
            pltpu.VMEM((32, 16, LANES), F32),
            dma((NI,)),
            dma((4,)),
            dma((4,)),
            dma((3,)),
            dma((3,)),
            dma((3,)),
            dma((3,)),
            dma,
            dma,
            dma((8,)),
            dma((8,)),
            dma,
            dma,
        ],
        compiler_params=pltpu.CompilerParams(collective_id=0, has_side_effects=True, vmem_limit_bytes=48 * 2**20),
        cost_estimate=pl.CostEstimate(flops=2**30, bytes_accessed=2**23, transcendentals=0),
    )(tensor, factor_b.T, factor_c)
    return a_rows, two.T.reshape(R, 1, 32)


def solution(mesh):
    placed = (P("ia", "ka", "ja"), P(("ja", "ka"), None), P("ka", None))
    return jax.shard_map(
        body,
        mesh=mesh,
        in_specs=placed,
        out_specs=(P(("ia", "ja", "ka"), None), P(None, "ja", ("ia", "ka"))),
        check_vma=False,
    )
```

time: 473 us -> 41.8 us (0.09)
  waiting for transfers between devices: 282 us -> 0 us
  blocking collectives: 124 us -> 0 us
  Pallas kernels: 0 us -> 38.2 us
  matrix products: 27 us -> 0 us
  other arithmetic: 16.1 us -> 0 us
  between operations: 14.8 us -> 0.65 us
    reduce_scatter x1 -> x0, waiting for transfers between devices: 282 us -> none  [body(): lax.psum_scatter(mode_partial, ('ia', 'ka'), scatter_dimension=1, tiled=T...]
    psum x2 -> x0, blocking collectives: 76.6 us -> none  [the longest x1 62.8 us: body(): gram_b = lax.psum(local_b, ('ja', 'ka'))]
    pallas_call x0 -> x1, Pallas kernels: none -> 38.2 us  [body(): pl.pallas_call(kernel, name='cp_step', out_shape=(jax.ShapeDtypeStruct((1...]
    unnamed x1 -> x0, blocking collectives: 31.1 us -> none
    dot_general x4 -> x0, matrix products: 26 us -> none  [the longest x1 14.4 us: body(): jnp.einsum('rij,jr->ir', partial_value, lax.all_gather(factor_b, 'ka', ax...]
    all_gather x1 -> x0, blocking collectives: 16.5 us -> none  [body(): lax.all_gather(factor_b, 'ka', axis=0, tiled=True)]
    another operation x5 -> x0, other arithmetic: 12.1 us -> none  [the longest x3 6.52 us: body(): triangle = jnp.linalg.cholesky(gram_b * gram_c)]
  transfers between devices with their start and end apart: 1 -> 0, of which waited for: 1 -> 0; matrix products, arithmetic and copies ran while one was open for 0% -> 0% of each run, Pallas kernels for 0% -> 0%
where the time goes in v1:
time: 41.8 us; the launch traced here: 41.7 us
  Pallas kernels  38.2 us (91%)
  local copies, waits for them, and re-layouts  2.77 us (7%)
  between operations  0.65 us (2%)
    pallas_call x1, Pallas kernels, body(): pl.pallas_call(kernel, name='cp_step', out_shape=(jax.ShapeDtypeStruct((1...  38.2 us
    unnamed x6, local copies, waits for them, and re-layouts  2.77 us

profile of v1, /device:TPU:1, one launch (start us, length us, event | category | flops | bytes accessed | tf_op | source)
XLA Modules:
  0.0 41.7 jit_solution(9456427855820947449)
XLA Ops:
  0.6 0.0 copy-start
  0.6 0.9 %copy-done = f32[512,64]{0,1:T(8,128)S(1)} copy-done((f32[512,64]{0,1:T(8,128)S(1)}, f32[512,64]{0,1:T(8,128)}, u32[]{:S(2)}) %copy-start) | copy-done | bytes 131096
  1.5 0.0 copy-start.1
  1.5 0.8 %copy-done.1 = f32[64,64]{1,0:T(8,128)S(1)} copy-done((f32[64,64]{1,0:T(8,128)S(1)}, f32[64,64]{1,0:T(8,128)}, u32[]{:S(2)}) %copy-start.1) | copy-done | bytes 16408
  2.3 38.2 %cp_step.1 = (f32[1,64]{1,0:T(1,128)S(1)}, f32[32,64]{1,0:T(8,128)S(1)}) custom-call(f32[16,64,2048]{2,1,0:T(8,128)} %tensor.1, f32[64,512]{1,0:T(8,128)S(1)} %bitcast.4, f32[64,64]{1,0:T(8,128)S(1)} %copy-done.1), custom_call_target="tpu_custom_call" | custom-call | flops 1073741824 | bytes 8388608 | tf_op jit(solution)/shard_map/cp_step/pallas_call | solution.py:323
  40.5 0.5 %copy.7 = f32[1,64]{1,0:T(1,128)} copy(f32[1,64]{1,0:T(1,128)S(1)} %get-tuple-element.8) | data formatting | bytes 512
  41.0 0.6 %copy.8 = f32[64,1,32]{0,2,1:T(8,128)} copy(f32[64,1,32]{0,2,1:T(8,128)S(1)} %bitcast.5) | data formatting | bytes 16384
Async XLA Ops:
  0.6 0.9 %copy-start = (f32[512,64]{0,1:T(8,128)S(1)}, f32[512,64]{0,1:T(8,128)}, u32[]{:S(2)}) copy-start(f32[512,64]{0,1:T(8,128)} %param.4) | copy-start | bytes 393220
  1.5 0.8 %copy-start.1 = (f32[64,64]{1,0:T(8,128)S(1)}, f32[64,64]{1,0:T(8,128)}, u32[]{:S(2)}) copy-start(f32[64,64]{1,0:T(8,128)} %c_ref.1) | copy-start | bytes 49156

commit v2 on v1

v2 whole, which is shorter than its diff:
```python
import jax
import jax.numpy as jnp
from jax import lax
from jax.experimental import pallas as pl
from jax.experimental.pallas import tpu as pltpu
from jax.sharding import PartitionSpec as P

MESH = pl.DeviceIdType.MESH
F32 = jnp.float32
BF16 = jnp.bfloat16
HIGHEST = lax.Precision.HIGHEST

R = 64
NI = 16
NK = 64
NT = 16
LANES = 128
NX, NY, NZ, NZLO = 4, 4, 8, 4
WITHIN = 2
NEAR = 2 * WITHIN + 1


def place(x, y, z, core):
    return (((z // NZLO) * NY + y) * 2 + core, x, z % NZLO)


def kernel(
    tensor,
    b_hbm,
    c_hbm,
    a_out,
    two_out,
    b_ref,
    c_ref,
    rows,
    partial,
    c_wide,
    gram_own,
    gram_x,
    gram_mid,
    gram_z,
    b_near,
    b_far,
    one_acc,
    one_own,
    one_recv,
    h_inv,
    a_wide,
    a_rows,
    pair_send,
    pair_recv,
    packed,
    near_recv,
    near_sum,
    last_recv,
    far_recv,
    in_sem,
    t_sem,
    b_send,
    b_recv_sem,
    gx_send,
    gx_recv,
    gz_send,
    gz_recv,
    one_send,
    one_recv_sem,
    pair_ssem,
    pair_rsem,
    near_send,
    near_rsem,
    last_send,
    last_rsem,
    far_send,
    far_rsem,
):
    ia = lax.axis_index("ia")
    x = lax.axis_index("ja")
    zlo = lax.axis_index("ka")
    core = ia % 2
    y = (ia // 2) % NY
    zhi = ia // (2 * NY)
    z = zhi * NZLO + zlo

    def at_z(d):
        return place(x, y, (z + d + NZ) % NZ, core)

    def at_x(d):
        return place((x + d) % NX, y, z, core)

    other_core = place(x, y, z, 1 - core)

    def remote(src, dst, send, recv, target):
        copy = pltpu.make_async_remote_copy(
            src_ref=src, dst_ref=dst, send_sem=send, recv_sem=recv, device_id=target, device_id_type=MESH
        )
        return copy

    def load_row(i):
        return pltpu.make_async_copy(tensor.at[i], rows.at[i], t_sem.at[i])

    load_c = pltpu.make_async_copy(c_hbm, c_ref, in_sem.at[0])
    load_b = pltpu.make_async_copy(b_hbm, b_ref, in_sem.at[1])
    load_c.start()
    load_b.start()
    for i in range(NI):
        load_row(i).start()

    barrier = pltpu.get_barrier_semaphore()
    peers = [other_core]
    peers += [at_x(d) for d in range(1, NX)]
    peers += [place(x, (y + d) % NY, z, core) for d in range(1, NY)]
    peers += [at_z(d) for d in range(1, NZ)]
    for peer in peers:
        pl.semaphore_signal(barrier, inc=1, device_id=peer, device_id_type=MESH)

    load_c.wait()
    c_t = c_ref[...].T
    c_hi = c_t.astype(BF16)
    c_lo = (c_t - c_hi.astype(F32)).astype(BF16)
    none = jnp.zeros_like(c_hi)
    for n, part in enumerate((c_hi, c_lo)):
        c_wide[n * 2 * R : n * 2 * R + R] = jnp.concatenate([part, part, none, none], axis=1)
        c_wide[n * 2 * R + R : (n + 1) * 2 * R] = jnp.concatenate([none, none, part, part], axis=1)
    def contract(i, carry):
        load_row(2 * i).wait()
        load_row(2 * i + 1).wait()
        for chunk in range(8):
            operand = []
            for n in range(2):
                values = rows[2 * i + n, :, pl.ds(chunk * 256, 256)]
                hi = values.astype(BF16)
                operand += [hi, (values - hi.astype(F32)).astype(BF16)]
            out = jnp.dot(c_wide[...], jnp.concatenate(operand, axis=0), preferred_element_type=F32)
            out = out[: 2 * R] + out[2 * R :]
            for part in range(2):
                for n in range(2):
                    piece = out[n * R : (n + 1) * R, part * LANES : (part + 1) * LANES]
                    partial[chunk * 2 + part, 2 * i + n] = piece
        return carry

    load_b.wait()
    pl.semaphore_wait(barrier, len(peers))

    half = b_ref.shape[1] // 2
    b_copies = [
        remote(b_ref.at[:, pl.ds(0, half)], b_far.at[0], b_send.at[2], b_recv_sem.at[2], at_z(2)),
        remote(b_ref.at[:, pl.ds(half, half)], b_far.at[1], b_send.at[3], b_recv_sem.at[3], at_z(-2)),
        remote(b_ref, b_near.at[0], b_send.at[0], b_recv_sem.at[0], at_z(1)),
        remote(b_ref, b_near.at[1], b_send.at[1], b_recv_sem.at[1], at_z(-1)),
    ]
    for copy in b_copies:
        copy.start()

    b_own = b_ref[...]
    gram_b = lax.dot_general(b_own, b_own, (((1,), (1,)), ((), ())), precision=HIGHEST, preferred_element_type=F32)
    gram_c = lax.dot_general(c_t, c_t, (((1,), (1,)), ((), ())), precision=HIGHEST, preferred_element_type=F32)
    gram_own[...] = jnp.concatenate([gram_b, gram_c], axis=1)

    gx_copies = [remote(gram_own, gram_x.at[d - 1], gx_send.at[d - 1], gx_recv.at[d - 1], at_x(d)) for d in (2, 1, 3)]
    for copy in gx_copies:
        copy.start()

    lax.fori_loop(0, NI // 2, contract, 0)

    for copy in gx_copies:
        copy.wait_recv()
    own = gram_own[...]
    total = own + gram_x[0] + gram_x[1] + gram_x[2]
    lane = lax.broadcasted_iota(jnp.int32, (R, LANES), 1)
    gram_mid[...] = jnp.where(lane < R, total, own)
    gz_copies = [
        remote(gram_mid, gram_z.at[n], gz_send.at[n], gz_recv.at[n], at_z(d)) for n, d in enumerate((2, 1, -1))
    ]
    for copy in gz_copies:
        copy.start()

    def first_block(i, carry):
        acc = jnp.zeros((R, LANES), F32)
        for part in range(4):
            acc += partial[zlo * 4 + part, i] * b_ref[:, part * LANES : (part + 1) * LANES]
        one_acc[i] = acc
        return carry

    lax.fori_loop(0, NI, first_block, 0)

    b_copies[2].wait_recv()
    b_copies[3].wait_recv()
    before = (zlo + 3) % NZLO
    after = (zlo + 1) % NZLO
    across = (zlo + 2) % NZLO

    def near_blocks(i, carry):
        acc = one_acc[i]
        for part in range(4):
            acc += partial[before * 4 + part, i] * b_near[0, :, part * LANES : (part + 1) * LANES]
            acc += partial[after * 4 + part, i] * b_near[1, :, part * LANES : (part + 1) * LANES]
        one_acc[i] = acc
        return carry

    lax.fori_loop(0, NI, near_blocks, 0)

    b_copies[0].wait_recv()
    b_copies[1].wait_recv()
    lane8 = lax.broadcasted_iota(jnp.int32, (8, LANES), 1)

    def far_block(i, carry):
        acc = one_acc[i]
        for part in range(4):
            acc += (
                partial[across * 4 + part, i]
                * b_far[part // 2, :, (part % 2) * LANES : (part % 2 + 1) * LANES]
            )
        for g in range(8):
            total = jnp.sum(acc[g * 8 : (g + 1) * 8], axis=1, keepdims=True)
            carry = jnp.where(lane8 == g * NI + i, total, carry)
        return carry

    one_own[...] = lax.fori_loop(0, NI, far_block, jnp.zeros((8, LANES), F32))

    one_targets = [((3 - n // NZLO), (3 - n % NZLO)) for n in range(NX * NZLO - 1)]
    for n, (dx, dz) in enumerate(one_targets):
        target = place((x + dx) % NX, y, zhi * NZLO + (zlo + dz) % NZLO, core)
        remote(one_own, one_recv.at[n], one_send, one_recv_sem, target).start()

    for copy in gz_copies:
        copy.wait_recv()
    grams = gram_mid[...] + gram_z[0] + gram_z[1] + gram_z[2]
    product = grams * pltpu.roll(grams, R, 1)
    row_id = lax.broadcasted_iota(jnp.int32, (R, LANES), 0)
    work = jnp.where(lane < R, product, jnp.where(lane == row_id + R, 1.0, 0.0))
    groups = [work[g * 8 : (g + 1) * 8] for g in range(8)]

    def wide(value):
        return jnp.broadcast_to(value, (8, LANES))

    sub = lax.broadcasted_iota(jnp.int32, (8, LANES), 0)
    for p in range(8):
        columns = {g: [wide(groups[g][:, p * 8 + j : p * 8 + j + 1]) for j in range(8)] for g in range(p, 8)}
        block = [[wide(columns[p][j][i : i + 1]) for j in range(i + 1)] for i in range(8)]
        scale = []
        for j in range(8):
            scale.append(lax.rsqrt(block[j][j]))
            for i in range(j + 1, 8):
                block[i][j] = block[i][j] * scale[j]
            for i in range(j + 1, 8):
                for k in range(j + 1, i + 1):
                    block[i][k] = block[i][k] - block[i][j] * block[k][j]
        units = []
        for j in range(8):
            unit = wide(groups[p][j : j + 1])
            for k in range(j):
                unit = unit - block[j][k] * units[k]
            units.append(unit * scale[j])
        done = units[0]
        for j in range(1, 8):
            done = jnp.where(sub == j, units[j], done)
        groups[p] = done
        for g in range(p + 1, 8):
            lower = []
            for j in range(8):
                column = columns[g][j]
                for k in range(j):
                    column = column - lower[k] * block[j][k]
                lower.append(column * scale[j])
                groups[g] = groups[g] - lower[j] * units[j]
    lower_inv = jnp.concatenate(groups, axis=0)[:, R:]
    h_inv[...] = lax.dot_general(
        lower_inv, lower_inv, (((0,), (0,)), ((), ())), precision=HIGHEST, preferred_element_type=F32
    )

    pltpu.make_async_copy(one_recv, one_recv, one_recv_sem).wait()
    mode_one = one_own[...]
    for n in range(NX * NZLO - 1):
        mode_one = mode_one + one_recv[n]
    mode_one_t = jnp.concatenate(
        [mode_one if g == 0 else pltpu.roll(mode_one, LANES - g * NI, 1) for g in range(8)], axis=0
    )
    a_t = jnp.dot(h_inv[...], mode_one_t, precision=HIGHEST, preferred_element_type=F32)
    for i in range(NI):
        a_wide[i] = jnp.broadcast_to(a_t[:, i : i + 1], (R, LANES))

    def combine(tiles):
        accs = [partial[tile, 0] * a_wide[0] for tile in tiles]
        for i in range(1, NI):
            wide_a = a_wide[i]
            accs = [acc + partial[tile, i] * wide_a for acc, tile in zip(accs, tiles)]
        return accs

    order = (2, 1, 3, 0)

    def tiles_of(dy, to_core):
        return [(to_zhi * NY + (y + dy) % NY) * 2 + to_core for to_zhi in range(2)]

    pair_copies = [
        remote(pair_send.at[n], pair_recv.at[n], pair_ssem.at[n], pair_rsem.at[n], other_core) for n in range(NY)
    ]
    for n, dy in enumerate(order):
        for to_zhi, value in enumerate(combine(tiles_of(dy, 1 - core))):
            pair_send[n, to_zhi] = value
        pair_copies[n].start()

    lane16 = lax.broadcasted_iota(jnp.int32, (16, LANES), 1) // 32
    near_copies, far_targets = [], []
    for n, dy in enumerate(order):
        values = combine(tiles_of(dy, core))
        pair_copies[n].wait_recv()
        for to_zhi in range(2):
            value = values[to_zhi] + pair_recv[n, to_zhi]
            for to_zlo in range(NZLO):
                block = value[0:16] if to_zlo == 0 else pltpu.roll(value[0:16], LANES - 32 * to_zlo, 1)
                for g in range(1, 4):
                    piece = value[g * 16 : (g + 1) * 16]
                    shift = (32 * (g - to_zlo)) % LANES
                    block = jnp.where(lane16 == g, pltpu.roll(piece, shift, 1) if shift else piece, block)
                packed[dy, (to_zhi * NZLO + to_zlo + WITHIN + NZ - z) % NZ] = block
        if dy:
            near = remote(
                packed.at[dy, pl.ds(0, NEAR)],
                near_recv.at[n],
                near_send.at[n],
                near_rsem.at[n],
                place(x, (y + dy) % NY, z, core),
            )
            near.start()
            near_copies.append(near)
        for e in range(NEAR, NZ):
            slot = n * (NZ - NEAR) + e - NEAR
            target = place(x, (y + dy) % NY, (z + e - WITHIN) % NZ, core)
            remote(packed.at[dy, e], far_recv.at[slot], far_send, far_rsem, target).start()

    a_rows[...] = a_t.T
    a_out[...] = a_rows[pl.ds(x * NZLO + zlo, 1), :]

    for copy in near_copies:
        copy.wait_recv()
    for e in range(NEAR):
        near_sum[e] = packed[0, e] + near_recv[0, e] + near_recv[1, e] + near_recv[2, e]
    last = [e for d in range(WITHIN, 0, -1) for e in (WITHIN + d, WITHIN - d)]
    last_copies = [
        remote(near_sum.at[e], last_recv.at[n], last_send.at[n], last_rsem.at[n], at_z(e - WITHIN))
        for n, e in enumerate(last)
    ]
    for copy in last_copies:
        copy.start()

    total = near_sum[WITHIN]
    pltpu.make_async_copy(far_recv, far_recv, far_rsem).wait()
    for n in range(NY * (NZ - NEAR)):
        total = total + far_recv[n]
    for n, copy in enumerate(last_copies):
        copy.wait_recv()
        total = total + last_recv[n]
    columns = jnp.concatenate([total if g == 0 else pltpu.roll(total, LANES - 32 * g, 1) for g in range(4)], axis=0)
    two_out[...] = columns.T[0:32]

    for copy in b_copies + gx_copies + gz_copies:
        copy.wait_send()
    pltpu.make_async_copy(one_recv, one_recv, one_send).wait()

    for copy in pair_copies + near_copies + last_copies:
        copy.wait_send()
    pltpu.make_async_copy(far_recv, far_recv, far_send).wait()


def body(tensor, factor_b, factor_c):
    dma = pltpu.SemaphoreType.DMA
    vmem = pl.BlockSpec(memory_space=pltpu.VMEM)
    hbm = pl.BlockSpec(memory_space=pltpu.HBM)
    a_rows, two = pl.pallas_call(
        kernel,
        name="cp_step",
        out_shape=(jax.ShapeDtypeStruct((1, R), F32), jax.ShapeDtypeStruct((32, R), F32)),
        in_specs=[hbm, hbm, hbm],
        out_specs=(vmem, vmem),
        scratch_shapes=[
            pltpu.VMEM((R, 512), F32),
            pltpu.VMEM((NK, R), F32),
            pltpu.VMEM((NI, NK, NT * LANES), F32),
            pltpu.VMEM((NT, NI, R, LANES), F32),
            pltpu.VMEM((4 * R, 4 * NK), BF16),
            pltpu.VMEM((R, LANES), F32),
            pltpu.VMEM((3, R, LANES), F32),
            pltpu.VMEM((R, LANES), F32),
            pltpu.VMEM((3, R, LANES), F32),
            pltpu.VMEM((2, R, 512), F32),
            pltpu.VMEM((2, R, 256), F32),
            pltpu.VMEM((NI, R, LANES), F32),
            pltpu.VMEM((8, LANES), F32),
            pltpu.VMEM((15, 8, LANES), F32),
            pltpu.VMEM((R, R), F32),
            pltpu.VMEM((NI, R, LANES), F32),
            pltpu.VMEM((LANES, R), F32),
            pltpu.VMEM((NY, 2, R, LANES), F32),
            pltpu.VMEM((NY, 2, R, LANES), F32),
            pltpu.VMEM((NY, NZ, 16, LANES), F32),
            pltpu.VMEM((NY - 1, NEAR, 16, LANES), F32),
            pltpu.VMEM((NEAR, 16, LANES), F32),
            pltpu.VMEM((NEAR - 1, 16, LANES), F32),
            pltpu.VMEM((NY * (NZ - NEAR), 16, LANES), F32),
            dma((2,)),
            dma((NI,)),
            dma((4,)),
            dma((4,)),
            dma((3,)),
            dma((3,)),
            dma((3,)),
            dma((3,)),
            dma,
            dma,
            dma((NY,)),
            dma((NY,)),
            dma((NY - 1,)),
            dma((NY - 1,)),
            dma((NEAR - 1,)),
            dma((NEAR - 1,)),
            dma,
            dma,
        ],
        compiler_params=pltpu.CompilerParams(collective_id=0, has_side_effects=True, vmem_limit_bytes=48 * 2**20),
        cost_estimate=pl.CostEstimate(flops=2**30, bytes_accessed=2**23, transcendentals=0),
    )(
        tensor,
        pltpu.with_memory_space_constraint(factor_b.T, pltpu.HBM),
        pltpu.with_memory_space_constraint(factor_c, pltpu.HBM),
    )
    return a_rows, two.T.reshape(R, 1, 32)


def solution(mesh):
    placed = (P("ia", "ka", "ja"), P(("ja", "ka"), None), P("ka", None))
    return jax.shard_map(
        body,
        mesh=mesh,
        in_specs=placed,
        out_specs=(P(("ia", "ja", "ka"), None), P(None, "ja", ("ia", "ka"))),
        check_vma=False,
    )
```

time: 41.8 us -> 38.7 us (0.926)
  local copies, waits for them, and re-layouts: 2.77 us -> 1.12 us
  Pallas kernels: 38.2 us -> 36.9 us
    unnamed x6 -> x2, local copies, waits for them, and re-layouts: 2.77 us -> 1.12 us
    pallas_call x1, Pallas kernels: 38.2 us -> 36.9 us  [body(): pl.pallas_call(kernel, name='cp_step', out_shape=(jax.ShapeDtypeStruct((1...]
where the time goes in v2:
time: 38.7 us; the launch traced here: 38.6 us
  Pallas kernels  36.9 us (95%)
  local copies, waits for them, and re-layouts  1.12 us (3%)
  between operations  0.64 us (2%)
    pallas_call x1, Pallas kernels, body(): pl.pallas_call(kernel, name='cp_step', out_shape=(jax.ShapeDtypeStruct((1...  36.9 us
    unnamed x2, local copies, waits for them, and re-layouts  1.12 us

profile of v2, /device:TPU:1, one launch (start us, length us, event | category | flops | bytes accessed | tf_op | source)
XLA Modules:
  0.0 38.6 jit_solution(15813896709293906478)
XLA Ops:
  0.6 36.9 %cp_step.1 = (f32[1,64]{1,0:T(1,128)S(1)}, f32[32,64]{1,0:T(8,128)S(1)}) custom-call(f32[16,64,2048]{2,1,0:T(8,128)} %tensor.1, f32[64,512]{1,0:T(8,128)} %bitcast.5, f32[64,64]{1,0:T(8,128)} %c_hbm.1), custom_call_target="tpu_custom_call" | custom-call | flops 1073741824 | bytes 8388608 | tf_op jit(solution)/shard_map/cp_step/pallas_call | solution.py:369
  37.5 0.5 %copy.7 = f32[1,64]{1,0:T(1,128)} copy(f32[1,64]{1,0:T(1,128)S(1)} %get-tuple-element.8) | data formatting | bytes 512
  38.0 0.6 %copy.8 = f32[64,1,32]{0,2,1:T(8,128)} copy(f32[64,1,32]{0,2,1:T(8,128)S(1)} %bitcast.4) | data formatting | bytes 16384

commit v3 on v2

--- a/solution.py
+++ b/solution.py
@@ -39,8 +39,8 @@
     gram_x,
     gram_mid,
     gram_z,
-    b_near,
-    b_far,
+    gram_sum,
+    b_in,
     one_acc,
     one_own,
     one_recv,
@@ -62,6 +62,8 @@
     gx_recv,
     gz_send,
     gz_recv,
+    gs_send,
+    gs_recv,
     one_send,
     one_recv_sem,
     pair_ssem,
@@ -142,12 +144,21 @@
     pl.semaphore_wait(barrier, len(peers))
 
     half = b_ref.shape[1] // 2
-    b_copies = [
-        remote(b_ref.at[:, pl.ds(0, half)], b_far.at[0], b_send.at[2], b_recv_sem.at[2], at_z(2)),
-        remote(b_ref.at[:, pl.ds(half, half)], b_far.at[1], b_send.at[3], b_recv_sem.at[3], at_z(-2)),
-        remote(b_ref, b_near.at[0], b_send.at[0], b_recv_sem.at[0], at_z(1)),
-        remote(b_ref, b_near.at[1], b_send.at[1], b_recv_sem.at[1], at_z(-1)),
-    ]
+    own_half = pl.ds(pl.multiple_of(core * half, half), half)
+    quarters = [pl.ds(pl.multiple_of(core * half + n * half // 2, half // 2), half // 2) for n in range(2)]
+    far_copies = [
+        remote(b_ref.at[:, quarters[n]], b_in.at[2, :, quarters[n]], b_send.at[2 + n], b_recv_sem.at[2 + n], at_z(d))
+        for n, d in enumerate((2, -2))
+    ]
+    near_b_copies = [
+        remote(b_ref.at[:, own_half], b_in.at[n, :, own_half], b_send.at[n], b_recv_sem.at[n], at_z(d))
+        for n, d in enumerate((1, -1))
+    ]
+    swap_copies = [
+        remote(b_in.at[n, :, own_half], b_in.at[n, :, own_half], b_send.at[4 + n], b_recv_sem.at[4 + n], other_core)
+        for n in range(3)
+    ]
+    b_copies = far_copies + near_b_copies
     for copy in b_copies:
         copy.start()
 
@@ -156,7 +167,8 @@
     gram_c = lax.dot_general(c_t, c_t, (((1,), (1,)), ((), ())), precision=HIGHEST, preferred_element_type=F32)
     gram_own[...] = jnp.concatenate([gram_b, gram_c], axis=1)
 
-    gx_copies = [remote(gram_own, gram_x.at[d - 1], gx_send.at[d - 1], gx_recv.at[d - 1], at_x(d)) for d in (2, 1, 3)]
+    own_rows = pl.ds(pl.multiple_of(core * (R // 2), R // 2), R // 2)
+    gx_copies = [remote(gram_own.at[own_rows], gram_x.at[d - 1], gx_send.at[d - 1], gx_recv.at[d - 1], at_x(d)) for d in (2, 1, 3)]
     for copy in gx_copies:
         copy.start()
 
@@ -164,10 +176,9 @@
 
     for copy in gx_copies:
         copy.wait_recv()
-    own = gram_own[...]
+    own = gram_own[own_rows, :]
     total = own + gram_x[0] + gram_x[1] + gram_x[2]
-    lane = lax.broadcasted_iota(jnp.int32, (R, LANES), 1)
-    gram_mid[...] = jnp.where(lane < R, total, own)
+    gram_mid[...] = jnp.where(lax.broadcasted_iota(jnp.int32, (R // 2, LANES), 1) < R, total, own)
     gz_copies = [
         remote(gram_mid, gram_z.at[n], gz_send.at[n], gz_recv.at[n], at_z(d)) for n, d in enumerate((2, 1, -1))
     ]
@@ -183,39 +194,40 @@
 
     lax.fori_loop(0, NI, first_block, 0)
 
-    b_copies[2].wait_recv()
-    b_copies[3].wait_recv()
-    before = (zlo + 3) % NZLO
-    after = (zlo + 1) % NZLO
-    across = (zlo + 2) % NZLO
-
-    def near_blocks(i, carry):
+    for copy in far_copies:
+        copy.wait_recv()
+    swap_copies[2].start()
+    for n in range(2):
+        near_b_copies[n].wait_recv()
+        swap_copies[n].start()
+    blocks = ((zlo + 3) % NZLO, (zlo + 1) % NZLO, (zlo + 2) % NZLO)
+
+    def half_blocks(i, to_core):
         acc = one_acc[i]
-        for part in range(4):
-            acc += partial[before * 4 + part, i] * b_near[0, :, part * LANES : (part + 1) * LANES]
-            acc += partial[after * 4 + part, i] * b_near[1, :, part * LANES : (part + 1) * LANES]
-        one_acc[i] = acc
+        for n in range(3):
+            for part in range(2):
+                start = pl.multiple_of(to_core * half + part * LANES, LANES)
+                acc += partial[blocks[n] * 4 + to_core * 2 + part, i] * b_in[n, :, pl.ds(start, LANES)]
+        return acc
+
+    def fetched_half(i, carry):
+        one_acc[i] = half_blocks(i, core)
         return carry
 
-    lax.fori_loop(0, NI, near_blocks, 0)
-
-    b_copies[0].wait_recv()
-    b_copies[1].wait_recv()
+    lax.fori_loop(0, NI, fetched_half, 0)
+
+    for copy in swap_copies:
+        copy.wait_recv()
     lane8 = lax.broadcasted_iota(jnp.int32, (8, LANES), 1)
 
-    def far_block(i, carry):
-        acc = one_acc[i]
-        for part in range(4):
-            acc += (
-                partial[across * 4 + part, i]
-                * b_far[part // 2, :, (part % 2) * LANES : (part % 2 + 1) * LANES]
-            )
+    def handed_half(i, carry):
+        acc = half_blocks(i, 1 - core)
         for g in range(8):
             total = jnp.sum(acc[g * 8 : (g + 1) * 8], axis=1, keepdims=True)
             carry = jnp.where(lane8 == g * NI + i, total, carry)
         return carry
 
-    one_own[...] = lax.fori_loop(0, NI, far_block, jnp.zeros((8, LANES), F32))
+    one_own[...] = lax.fori_loop(0, NI, handed_half, jnp.zeros((8, LANES), F32))
 
     one_targets = [((3 - n // NZLO), (3 - n % NZLO)) for n in range(NX * NZLO - 1)]
     for n, (dx, dz) in enumerate(one_targets):
@@ -224,7 +236,12 @@
 
     for copy in gz_copies:
         copy.wait_recv()
-    grams = gram_mid[...] + gram_z[0] + gram_z[1] + gram_z[2]
+    gram_sum[own_rows, :] = gram_mid[...] + gram_z[0] + gram_z[1] + gram_z[2]
+    g_swap = remote(gram_sum.at[own_rows], gram_sum.at[own_rows], gs_send, gs_recv, other_core)
+    g_swap.start()
+    g_swap.wait_recv()
+    grams = gram_sum[...]
+    lane = lax.broadcasted_iota(jnp.int32, (R, LANES), 1)
     product = grams * pltpu.roll(grams, R, 1)
     row_id = lax.broadcasted_iota(jnp.int32, (R, LANES), 0)
     work = jnp.where(lane < R, product, jnp.where(lane == row_id + R, 1.0, 0.0))
@@ -353,7 +370,7 @@
     columns = jnp.concatenate([total if g == 0 else pltpu.roll(total, LANES - 32 * g, 1) for g in range(4)], axis=0)
     two_out[...] = columns.T[0:32]
 
-    for copy in b_copies + gx_copies + gz_copies:
+    for copy in b_copies + swap_copies + gx_copies + gz_copies + [g_swap]:
         copy.wait_send()
     pltpu.make_async_copy(one_recv, one_recv, one_send).wait()
 
@@ -379,11 +396,11 @@
             pltpu.VMEM((NT, NI, R, LANES), F32),
             pltpu.VMEM((4 * R, 4 * NK), BF16),
             pltpu.VMEM((R, LANES), F32),
-            pltpu.VMEM((3, R, LANES), F32),
+            pltpu.VMEM((3, R // 2, LANES), F32),
+            pltpu.VMEM((R // 2, LANES), F32),
+            pltpu.VMEM((3, R // 2, LANES), F32),
             pltpu.VMEM((R, LANES), F32),
-            pltpu.VMEM((3, R, LANES), F32),
-            pltpu.VMEM((2, R, 512), F32),
-            pltpu.VMEM((2, R, 256), F32),
+            pltpu.VMEM((3, R, 512), F32),
             pltpu.VMEM((NI, R, LANES), F32),
             pltpu.VMEM((8, LANES), F32),
             pltpu.VMEM((15, 8, LANES), F32),
@@ -399,12 +416,14 @@
             pltpu.VMEM((NY * (NZ - NEAR), 16, LANES), F32),
             dma((2,)),
             dma((NI,)),
-            dma((4,)),
-            dma((4,)),
+            dma((7,)),
+            dma((7,)),
             dma((3,)),
             dma((3,)),
             dma((3,)),
             dma((3,)),
+            dma,
+            dma,
             dma,
             dma,
             dma((NY,)),

time: 38.7 us -> 36 us (0.930)
  Pallas kernels: 36.9 us -> 34.2 us
    pallas_call x1, Pallas kernels: 36.9 us -> 34.2 us  [body(): pl.pallas_call(kernel, name='cp_step', out_shape=(jax.ShapeDtypeStruct((1...]
where the time goes in v3:
time: 36 us; the launch traced here: 35.9 us
  Pallas kernels  34.2 us (95%)
  local copies, waits for them, and re-layouts  1.12 us (3%)
  between operations  0.64 us (2%)
    pallas_call x1, Pallas kernels, body(): pl.pallas_call(kernel, name='cp_step', out_shape=(jax.ShapeDtypeStruct((1...  34.2 us
    unnamed x2, local copies, waits for them, and re-layouts  1.12 us

profile of v3, /device:TPU:1, one launch (start us, length us, event | category | flops | bytes accessed | tf_op | source)
XLA Modules:
  0.0 35.9 jit_solution(460398240773377982)
XLA Ops:
  0.6 34.2 %cp_step.1 = (f32[1,64]{1,0:T(1,128)S(1)}, f32[32,64]{1,0:T(8,128)S(1)}) custom-call(f32[16,64,2048]{2,1,0:T(8,128)} %tensor.1, f32[64,512]{1,0:T(8,128)} %bitcast.5, f32[64,64]{1,0:T(8,128)} %c_hbm.1), custom_call_target="tpu_custom_call" | custom-call | flops 1073741824 | bytes 8388608 | tf_op jit(solution)/shard_map/cp_step/pallas_call | solution.py:386
  34.8 0.5 %copy.7 = f32[1,64]{1,0:T(1,128)} copy(f32[1,64]{1,0:T(1,128)S(1)} %get-tuple-element.8) | data formatting | bytes 512
  35.3 0.6 %copy.8 = f32[64,1,32]{0,2,1:T(8,128)} copy(f32[64,1,32]{0,2,1:T(8,128)S(1)} %bitcast.4) | data formatting | bytes 16384

commit v4 on v3

--- a/solution.py
+++ b/solution.py
@@ -83,6 +83,9 @@
     zhi = ia // (2 * NY)
     z = zhi * NZLO + zlo
 
+    xs = [x] + [lax.rem(x + d, NX) for d in range(1, NX)]
+    zlos = [zlo] + [lax.rem(zlo + d, NZLO) for d in range(1, NZLO)]
+
     def at_z(d):
         return place(x, y, (z + d + NZ) % NZ, core)
 
@@ -172,7 +175,7 @@
     for copy in gx_copies:
         copy.start()
 
-    lax.fori_loop(0, NI // 2, contract, 0)
+    lax.fori_loop(0, NI // 2, contract, 0, unroll=2)
 
     for copy in gx_copies:
         copy.wait_recv()
@@ -192,7 +195,7 @@
         one_acc[i] = acc
         return carry
 
-    lax.fori_loop(0, NI, first_block, 0)
+    lax.fori_loop(0, NI, first_block, 0, unroll=4)
 
     for copy in far_copies:
         copy.wait_recv()
@@ -214,7 +217,7 @@
         one_acc[i] = half_blocks(i, core)
         return carry
 
-    lax.fori_loop(0, NI, fetched_half, 0)
+    lax.fori_loop(0, NI, fetched_half, 0, unroll=4)
 
     for copy in swap_copies:
         copy.wait_recv()
@@ -227,11 +230,11 @@
             carry = jnp.where(lane8 == g * NI + i, total, carry)
         return carry
 
-    one_own[...] = lax.fori_loop(0, NI, handed_half, jnp.zeros((8, LANES), F32))
-
-    one_targets = [((3 - n // NZLO), (3 - n % NZLO)) for n in range(NX * NZLO - 1)]
+    one_own[...] = lax.fori_loop(0, NI, handed_half, jnp.zeros((8, LANES), F32), unroll=4)
+
+    one_targets = [(dx, dz) for dz in (3, 1, 2) for dx in (2, 1, 3)] + [(0, 3), (0, 1), (2, 0), (0, 2), (1, 0), (3, 0)]
     for n, (dx, dz) in enumerate(one_targets):
-        target = place((x + dx) % NX, y, zhi * NZLO + (zlo + dz) % NZLO, core)
+        target = (ia, xs[dx], zlos[dz])
         remote(one_own, one_recv.at[n], one_send, one_recv_sem, target).start()
 
     for copy in gz_copies:

time: 36 us -> 33.7 us (0.936)
  Pallas kernels: 34.2 us -> 31.8 us
    pallas_call x1, Pallas kernels: 34.2 us -> 31.8 us  [body(): pl.pallas_call(kernel, name='cp_step', out_shape=(jax.ShapeDtypeStruct((1...]
where the time goes in v4:
time: 33.7 us; the launch traced here: 33.6 us
  Pallas kernels  31.8 us (94%)
  local copies, waits for them, and re-layouts  1.12 us (3%)
  between operations  0.64 us (2%)
    pallas_call x1, Pallas kernels, body(): pl.pallas_call(kernel, name='cp_step', out_shape=(jax.ShapeDtypeStruct((1...  31.8 us
    unnamed x2, local copies, waits for them, and re-layouts  1.12 us

profile of v4, /device:TPU:1, one launch (start us, length us, event | category | flops | bytes accessed | tf_op | source)
XLA Modules:
  0.0 33.6 jit_solution(7793498403921489635)
XLA Ops:
  0.6 31.8 %cp_step.1 = (f32[1,64]{1,0:T(1,128)S(1)}, f32[32,64]{1,0:T(8,128)S(1)}) custom-call(f32[16,64,2048]{2,1,0:T(8,128)} %tensor.1, f32[64,512]{1,0:T(8,128)} %bitcast.5, f32[64,64]{1,0:T(8,128)} %c_hbm.1), custom_call_target="tpu_custom_call" | custom-call | flops 1073741824 | bytes 8388608 | tf_op jit(solution)/shard_map/cp_step/pallas_call | solution.py:389
  32.5 0.5 %copy.7 = f32[1,64]{1,0:T(1,128)} copy(f32[1,64]{1,0:T(1,128)S(1)} %get-tuple-element.8) | data formatting | bytes 512
  33.0 0.6 %copy.8 = f32[64,1,32]{0,2,1:T(8,128)} copy(f32[64,1,32]{0,2,1:T(8,128)S(1)} %bitcast.4) | data formatting | bytes 16384

commit v5 on v4

--- a/solution.py
+++ b/solution.py
@@ -86,6 +86,11 @@
     xs = [x] + [lax.rem(x + d, NX) for d in range(1, NX)]
     zlos = [zlo] + [lax.rem(zlo + d, NZLO) for d in range(1, NZLO)]
 
+    ys = [y] + [lax.rem(y + d, NY) for d in range(1, NY)]
+    zs = [z] + [lax.rem(z + d, NZ) for d in range(1, NZ)]
+    zhis = [lax.div(v, NZLO) for v in zs]
+    zls = [lax.rem(v, NZLO) for v in zs]
+
     def at_z(d):
         return place(x, y, (z + d + NZ) % NZ, core)
 
@@ -118,14 +123,6 @@
     for peer in peers:
         pl.semaphore_signal(barrier, inc=1, device_id=peer, device_id_type=MESH)
 
-    load_c.wait()
-    c_t = c_ref[...].T
-    c_hi = c_t.astype(BF16)
-    c_lo = (c_t - c_hi.astype(F32)).astype(BF16)
-    none = jnp.zeros_like(c_hi)
-    for n, part in enumerate((c_hi, c_lo)):
-        c_wide[n * 2 * R : n * 2 * R + R] = jnp.concatenate([part, part, none, none], axis=1)
-        c_wide[n * 2 * R + R : (n + 1) * 2 * R] = jnp.concatenate([none, none, part, part], axis=1)
     def contract(i, carry):
         load_row(2 * i).wait()
         load_row(2 * i + 1).wait()
@@ -165,6 +162,14 @@
     for copy in b_copies:
         copy.start()
 
+    load_c.wait()
+    c_t = c_ref[...].T
+    c_hi = c_t.astype(BF16)
+    c_lo = (c_t - c_hi.astype(F32)).astype(BF16)
+    none = jnp.zeros_like(c_hi)
+    for n, part in enumerate((c_hi, c_lo)):
+        c_wide[n * 2 * R : n * 2 * R + R] = jnp.concatenate([part, part, none, none], axis=1)
+        c_wide[n * 2 * R + R : (n + 1) * 2 * R] = jnp.concatenate([none, none, part, part], axis=1)
     b_own = b_ref[...]
     gram_b = lax.dot_general(b_own, b_own, (((1,), (1,)), ((), ())), precision=HIGHEST, preferred_element_type=F32)
     gram_c = lax.dot_general(c_t, c_t, (((1,), (1,)), ((), ())), precision=HIGHEST, preferred_element_type=F32)
@@ -195,7 +200,7 @@
         one_acc[i] = acc
         return carry
 
-    lax.fori_loop(0, NI, first_block, 0, unroll=4)
+    lax.fori_loop(0, NI, first_block, 0, unroll=8)
 
     for copy in far_copies:
         copy.wait_recv()
@@ -217,7 +222,7 @@
         one_acc[i] = half_blocks(i, core)
         return carry
 
-    lax.fori_loop(0, NI, fetched_half, 0, unroll=4)
+    lax.fori_loop(0, NI, fetched_half, 0, unroll=8)
 
     for copy in swap_copies:
         copy.wait_recv()
@@ -230,7 +235,7 @@
             carry = jnp.where(lane8 == g * NI + i, total, carry)
         return carry
 
-    one_own[...] = lax.fori_loop(0, NI, handed_half, jnp.zeros((8, LANES), F32), unroll=4)
+    one_own[...] = lax.fori_loop(0, NI, handed_half, jnp.zeros((8, LANES), F32), unroll=8)
 
     one_targets = [(dx, dz) for dz in (3, 1, 2) for dx in (2, 1, 3)] + [(0, 3), (0, 1), (2, 0), (0, 2), (1, 0), (3, 0)]
     for n, (dx, dz) in enumerate(one_targets):
@@ -309,7 +314,7 @@
     order = (2, 1, 3, 0)
 
     def tiles_of(dy, to_core):
-        return [(to_zhi * NY + (y + dy) % NY) * 2 + to_core for to_zhi in range(2)]
+        return [(to_zhi * NY + ys[dy]) * 2 + to_core for to_zhi in range(2)]
 
     pair_copies = [
         remote(pair_send.at[n], pair_recv.at[n], pair_ssem.at[n], pair_rsem.at[n], other_core) for n in range(NY)
@@ -332,7 +337,7 @@
                     piece = value[g * 16 : (g + 1) * 16]
                     shift = (32 * (g - to_zlo)) % LANES
                     block = jnp.where(lane16 == g, pltpu.roll(piece, shift, 1) if shift else piece, block)
-                packed[dy, (to_zhi * NZLO + to_zlo + WITHIN + NZ - z) % NZ] = block
+                packed[dy, lax.rem(to_zhi * NZLO + to_zlo + WITHIN + NZ - z, NZ)] = block
         if dy:
             near = remote(
                 packed.at[dy, pl.ds(0, NEAR)],
@@ -345,7 +350,7 @@
             near_copies.append(near)
         for e in range(NEAR, NZ):
             slot = n * (NZ - NEAR) + e - NEAR
-            target = place(x, (y + dy) % NY, (z + e - WITHIN) % NZ, core)
+            target = ((zhis[(e - WITHIN) % NZ] * NY + ys[dy]) * 2 + core, x, zls[(e - WITHIN) % NZ])
             remote(packed.at[dy, e], far_recv.at[slot], far_send, far_rsem, target).start()
 
     a_rows[...] = a_t.T

time: 33.7 us -> 33.8 us (level)
  no operation moved by 1% of the time
where the time goes in v5:
time: 33.8 us
  Pallas kernels  32 us (95%)
  local copies, waits for them, and re-layouts  1.12 us (3%)
  between operations  0.64 us (2%)
    pallas_call x1, Pallas kernels, body(): pl.pallas_call(kernel, name='cp_step', out_shape=(jax.ShapeDtypeStruct((1...  32 us
    unnamed x2, local copies, waits for them, and re-layouts  1.12 us

profile of v5, /device:TPU:1, one launch (start us, length us, event | category | flops | bytes accessed | tf_op | source)
XLA Modules:
  0.0 33.8 jit_solution(16580111559065217202)
XLA Ops:
  0.6 32.0 %cp_step.1 = (f32[1,64]{1,0:T(1,128)S(1)}, f32[32,64]{1,0:T(8,128)S(1)}) custom-call(f32[16,64,2048]{2,1,0:T(8,128)} %tensor.1, f32[64,512]{1,0:T(8,128)} %bitcast.5, f32[64,64]{1,0:T(8,128)} %c_hbm.1), custom_call_target="tpu_custom_call" | custom-call | flops 1073741824 | bytes 8388608 | tf_op jit(solution)/shard_map/cp_step/pallas_call | solution.py:394
  32.7 0.5 %copy.7 = f32[1,64]{1,0:T(1,128)} copy(f32[1,64]{1,0:T(1,128)S(1)} %get-tuple-element.8) | data formatting | bytes 512
  33.2 0.6 %copy.8 = f32[64,1,32]{0,2,1:T(8,128)} copy(f32[64,1,32]{0,2,1:T(8,128)S(1)} %bitcast.4) | data formatting | bytes 16384
